TPU v7x, 32 devices: a whole 2x2x4 slice. The times are simulated.
32 devices in a mesh: row: 8 (over y, x, core), col: 4 (over z).
Axes of the slice: x: 2, y: 2, z: 4, core: 2. Of those that a mesh axis runs over, the one named last changes fastest.
Arguments:
- u_factors: bfloat16 [24, 24, 1024, 128], P('row', 'col'), may hold values from -0.109375 to 0.109375
- v_factors: bfloat16 [24, 24, 1024, 128], P('row', 'col'), may hold values from -0.1875 to 0.1875
- tile_scales: float32 [24, 24, 128], P('row', 'col'), may hold values from 0.3 to 3
- rank_class: int32 [24, 24], P('row', 'col'), may hold values from 0 to 3, as said below
- slopes: float32 [64, 24576], P(None, 'row'), may hold values from -40 to 40
Outputs:
- solution_field: float32 [64, 24576], P(None, 'col')
- residual: float32 [64, 24576], P(None, 'col')
Inputs may be any that keep to these rules, and one draw needn't show every extreme that they name: `rank_class`: class k gives a tile of rank 128 / 8 * 2**k; tiles of one device tend to share high or low classes.
All inputs are finite; a program needn't handle non-finite values.
Results may differ from a plain program's by a relative error of at most 0.017.
Values may be sent and summed in bfloat16 or wider, within the bound.
A program may use at most 64 MiB of HBM per device.

v0:
```python
import jax
import jax.numpy as jnp
from jax import lax
from jax.sharding import PartitionSpec as P

ITERS = 2


damping = 0.1
epsilon = 1e-06


def rank_weights(tile_scales, rank_class):
    max_rank = tile_scales.shape[-1]
    ranks = jnp.left_shift(jnp.int32(max_rank // 8), rank_class)
    columns = lax.broadcasted_iota(jnp.int32, tile_scales.shape, 2)
    return jnp.where(columns < ranks[:, :, None], tile_scales, jnp.zeros_like(tile_scales))


def padded_apply(source, first_factor, second_factor, weights, transpose):
    rows_here, cols_here, tile_size, max_rank = first_factor.shape
    frames = source.shape[0]
    if transpose:
        pieces = source.reshape(frames, rows_here, tile_size)
        projected = jnp.einsum(
            "fis,ijsr->fijr", pieces, first_factor, preferred_element_type=jnp.float32
        )
        scaled = (projected * weights[None]).astype(jnp.bfloat16)
        result = jnp.einsum(
            "fijr,ijmr->fjm", scaled, second_factor, preferred_element_type=jnp.float32
        )
        return result.reshape(frames, cols_here * tile_size)
    pieces = source.reshape(frames, cols_here, tile_size)
    projected = jnp.einsum(
        "fjm,ijmr->fijr", pieces, first_factor, preferred_element_type=jnp.float32
    )
    scaled = (projected * weights[None]).astype(jnp.bfloat16)
    result = jnp.einsum("fijr,ijsr->fis", scaled, second_factor, preferred_element_type=jnp.float32)
    return result.reshape(frames, rows_here * tile_size)


def apply_tiles(source, first_factor, second_factor, weights, transpose):
    return padded_apply(source, first_factor, second_factor, weights, transpose)


def per_device(u_factors, v_factors, tile_scales, rank_class, slopes):
    weights = rank_weights(tile_scales, rank_class)
    rows_here, cols_here, tile_size, max_rank = u_factors.shape
    share_width = cols_here * tile_size // lax.axis_size("row")
    offset = lax.axis_index("row") * share_width

    def backward(image_b):
        partial_value = apply_tiles(image_b, u_factors, v_factors, weights, True)
        return lax.psum(partial_value, "row")

    def own_part(field):
        return lax.dynamic_slice_in_dim(field, offset, share_width, 1)

    def frame_product(left_field, right_field):
        return jnp.sum(own_part(left_field) * own_part(right_field), axis=1)

    right_side = backward(slopes.astype(jnp.bfloat16))
    solution_field = jnp.zeros_like(right_side)
    residual = right_side
    direction = right_side
    norm_now = lax.psum(frame_product(residual, residual), ("row", "col"))
    dir_norm = norm_now
    for sweep in range(ITERS):
        narrowed = direction.astype(jnp.bfloat16)
        forward_partial_value = apply_tiles(narrowed, v_factors, u_factors, weights, False)
        forward_image = lax.psum(forward_partial_value, "col")
        image_norm = lax.psum(jnp.sum(forward_image * forward_image, axis=1), "row")
        dir_norm = lax.psum(frame_product(direction, direction), ("row", "col"))
        operator_image = backward(forward_image.astype(jnp.bfloat16)) + damping * direction
        step_size = norm_now / (image_norm + damping * dir_norm + epsilon)
        solution_field = solution_field + step_size[:, None] * direction
        residual = residual - step_size[:, None] * operator_image
        if sweep + 1 < ITERS:
            norm_next = lax.psum(frame_product(residual, residual), ("row", "col"))
            growth = norm_next / (norm_now + epsilon)
            direction = residual + growth[:, None] * direction
            norm_now = norm_next
    return (solution_field, residual)


def solution(mesh):
    return jax.shard_map(
        per_device,
        mesh=mesh,
        in_specs=(
            P("row", "col", None, None),
            P("row", "col", None, None),
            P("row", "col", None),
            P("row", "col"),
            P(None, "row"),
        ),
        out_specs=(P(None, "col"), P(None, "col")),
        check_vma=False,
    )
```

profile of v0, /device:TPU:0, one launch (start us, length us, event | category | flops | bytes accessed | tf_op | source)
XLA Modules:
  0.0 383.3 jit_solution(15641545947727971645)
XLA Ops:
  10.4 6.1 %fusion.12 = f32[6,8,8,1024]{3,2,1,0:T(8,128)S(1)} fusion(bf16[3,6,1024,128]{3,2,1,0:T(8,128)(2,1)} %param.6, bf16[3,6,1024,128]{3,2,1,0:T(8,128)(2,1)} %param.5, bf16[64,3,1024,1]{2,1,0,3:T(4,128)(2,1)S(1)} %reshape.49, f32[3,6,128]{2,0,1:T(4,128)S(1)} %copy.12), kind=kOutput, calls=%fused_computation.16 | convolution fusion | flops 604274688 | bytes 11412480 | tf_op jit(solution)/shard_map/fijr,ijmr->fjm/dot_general | solution.py:29
  17.9 61.8 %all-reduce.6.cloned.1.call-done = f32[64,6144]{1,0:T(8,128)} async-done(((f32[64,6144]{1,0:T(8,128)}), f32[64,6144]{1,0:T(8,128)}) %all-reduce.6.cloned.1.call-update) | async-done | bytes 1572880 | tf_op jit(solution)/shard_map/psum | solution.py:54
  79.7 1.5 convert_element_type.42
  82.2 6.6 %convolution_bitcast_fusion.1 = f32[3,8,8,1024]{3,2,1,0:T(8,128)S(1)} fusion(bf16[3,6,1024,128]{3,2,1,0:T(8,128)(2,1)} %param.5, bf16[3,6,1024,128]{3,2,1,0:T(8,128)(2,1)} %param.6, bf16[64,6,1024,1]{2,1,0,3:T(8,128)(2,1)S(1)} %reshape.51, f32[3,6,128]{2,1,0:T(8,128)S(1)} %fusion.73), kind=kOutput, calls=%fused_computation.20 | convolution fusion | flops 604274688 | bytes 11019264 | tf_op jit(solution)/shard_map/fijr,ijsr->fis/dot_general | solution.py:38
  89.7 43.1 %all-reduce.8.cloned.1.call-done = f32[64,3072]{1,0:T(8,128)} async-done(((f32[64,3072]{1,0:T(8,128)}), f32[64,3072]{1,0:T(8,128)}) %all-reduce.8.cloned.1.call-update) | async-done | bytes 786448 | tf_op jit(solution)/shard_map/psum | solution.py:71
  132.9 1.6 multiply_reduce_fusion.1
  135.0 6.1 %fusion.15 = f32[6,8,8,1024]{3,2,1,0:T(8,128)S(1)} fusion(bf16[3,6,1024,128]{3,2,1,0:T(8,128)(2,1)} %param.6, bf16[3,6,1024,128]{3,2,1,0:T(8,128)(2,1)} %param.5, bf16[64,3,1024,1]{2,1,0,3:T(4,128)(2,1)S(1)} %reshape.53, f32[3,6,128]{2,0,1:T(4,128)S(1)} %copy.12), kind=kOutput, calls=%fused_computation.17 | convolution fusion | flops 604274688 | bytes 11412480 | tf_op jit(solution)/shard_map/fijr,ijmr->fjm/dot_general | solution.py:29
  143.9 39.8 %psum.74 = f32[64]{0:T(128)S(1)} all-reduce(f32[64]{0:T(128)S(1)} %multiply_reduce_fusion.4), channel_id=1, replica_groups=mesh['row'=8,'col'=4] {'row','col'}, use_global_device_ids=true, to_apply=%region_2.3 | all-reduce | flops 64 | bytes 512 | tf_op jit(solution)/shard_map/psum | solution.py:66
  183.8 12.9 %psum.76 = f32[64]{0:T(128)S(1)} all-reduce(f32[64]{0:T(128)S(1)} %get-tuple-element.8), channel_id=1, replica_groups=mesh['row'=8,'col'=4] {'row'}, use_global_device_ids=true, to_apply=%region_5.6 | all-reduce | flops 64 | bytes 512 | tf_op jit(solution)/shard_map/psum | solution.py:72
  196.7 4.7 %all-reduce.10.cloned.1.call-done = f32[64,6144]{1,0:T(8,128)} async-done(((f32[64,6144]{1,0:T(8,128)}), f32[64,6144]{1,0:T(8,128)}) %all-reduce.10.cloned.1.call-update) | async-done | bytes 1572880 | tf_op jit(solution)/shard_map/psum | solution.py:54
  201.4 1.7 multiply_subtract_fusion.1
  203.2 39.7 %psum.78 = f32[64]{0:T(128)S(1)} all-reduce(f32[64]{0:T(128)S(1)} %multiply_reduce_fusion.3), channel_id=1, replica_groups=mesh['row'=8,'col'=4] {'row','col'}, use_global_device_ids=true, to_apply=%region_8.9 | all-reduce | flops 64 | bytes 512 | tf_op jit(solution)/shard_map/psum | solution.py:79
  242.8 1.7 fusion.74
  244.5 2.8 reshape.55
  247.3 7.7 %convolution_bitcast_fusion = f32[3,8,8,1024]{3,2,1,0:T(8,128)} fusion(bf16[3,6,1024,128]{3,2,1,0:T(8,128)(2,1)} %param.5, bf16[3,6,1024,128]{3,2,1,0:T(8,128)(2,1)} %param.6, bf16[64,6,1024,1]{2,1,0,3:T(8,128)(2,1)} %reshape.55, f32[3,6,128]{2,1,0:T(8,128)S(1)} %fusion.73), kind=kOutput, calls=%fused_computation.19 | convolution fusion | flops 604274688 | bytes 11019264 | tf_op jit(solution)/shard_map/fijr,ijsr->fis/dot_general | solution.py:38
  255.1 2.1 copy.36
  257.2 43.6 %all-reduce.12.cloned.1.call-done = f32[64,3072]{1,0:T(8,128)} async-done(((f32[64,3072]{1,0:T(8,128)}), f32[64,3072]{1,0:T(8,128)}) %all-reduce.12.cloned.1.call-update) | async-done | bytes 786448 | tf_op jit(solution)/shard_map/psum | solution.py:71
  300.8 2.1 fusion.75
  304.1 7.4 %fusion.18 = f32[6,8,8,1024]{3,2,1,0:T(8,128)} fusion(bf16[3,6,1024,128]{3,2,1,0:T(8,128)(2,1)} %param.6, bf16[3,6,1024,128]{3,2,1,0:T(8,128)(2,1)} %param.5, bf16[64,3,1024,1]{2,1,0,3:T(4,128)(2,1)} %reshape.57, f32[3,6,128]{2,0,1:T(4,128)S(1)} %copy.12), kind=kOutput, calls=%fused_computation.18 | convolution fusion | flops 604274688 | bytes 11412480 | tf_op jit(solution)/shard_map/fijr,ijmr->fjm/dot_general | solution.py:29
  311.5 2.7 copy.37
  315.3 40.0 %psum.81 = f32[64]{0:T(128)S(1)} all-reduce(f32[64]{0:T(128)S(1)} %multiply_reduce_fusion.2), channel_id=1, replica_groups=mesh['row'=8,'col'=4] {'row','col'}, use_global_device_ids=true, to_apply=%region_13.14 | all-reduce | flops 64 | bytes 512 | tf_op jit(solution)/shard_map/psum | solution.py:73
  355.3 12.9 %psum.80 = f32[64]{0:T(128)S(1)} all-reduce(f32[64]{0:T(128)S(1)} %copy-done.1), channel_id=1, replica_groups=mesh['row'=8,'col'=4] {'row'}, use_global_device_ids=true, to_apply=%region_11.12 | all-reduce | flops 64 | bytes 512 | tf_op jit(solution)/shard_map/psum | solution.py:72
  368.2 4.6 %all-reduce.14.cloned.1.call-done = f32[64,6144]{1,0:T(8,128)} async-done(((f32[64,6144]{1,0:T(8,128)}), f32[64,6144]{1,0:T(8,128)}) %all-reduce.14.cloned.1.call-update) | async-done | bytes 1572880 | tf_op jit(solution)/shard_map/psum | solution.py:54
  372.8 4.0 %multiply_subtract_fusion = (f32[64,6144]{1,0:T(8,128)}, f32[64,6144]{1,0:T(8,128)}) fusion(f32[64,6144]{1,0:T(8,128)S(1)} %multiply_subtract_fusion.1, f32[64,6144]{1,0:T(8,128)} %all-reduce.14.cloned.1.call-done, f32[64,6144]{1,0:T(8,128)} %get-tuple-element.3, f32[64]{0:T(128)S(1)} %add_divide_fusion, f32[64,6144]{1,0:T(8,128)S(1)} %copy-done, ...), kind=kLoop, calls=%fused_computation.12 | loop fusion | flops 2752512 | bytes 9437696 | tf_op jit(solution)/shard_map/sub | solution.py:77
  (35 shorter events, 12.5 us)
Async XLA Ops:
  7.2 72.5 %all-reduce.6.cloned.1.call-start = ((), (), s32[]{:S(2)}) async-start(), calls=%async_computation | async-start | bytes 3145728 | tf_op jit(solution)/shard_map/psum | solution.py:54
  17.9 115.0 %all-reduce.8.cloned.1.call-start = ((), (), s32[]{:S(2)}) async-start(), calls=%async_computation.1 | async-start | bytes 1572864 | tf_op jit(solution)/shard_map/psum | solution.py:71
  89.7 111.7 %all-reduce.10.cloned.1.call-start = ((), (), s32[]{:S(2)}) async-start(), calls=%async_computation.2 | async-start | bytes 3145728 | tf_op jit(solution)/shard_map/psum | solution.py:54
  142.4 1.4 copy-start
  142.4 158.4 %all-reduce.12.cloned.1.call-start = ((), (), s32[]{:S(2)}) async-start(), calls=%async_computation.3 | async-start | bytes 1572864 | tf_op jit(solution)/shard_map/psum | solution.py:71
  242.8 1.7 copy-start.2
  257.2 115.6 %all-reduce.14.cloned.1.call-start = ((), (), s32[]{:S(2)}) async-start(), calls=%async_computation.4 | async-start | bytes 3145728 | tf_op jit(solution)/shard_map/psum | solution.py:54
  314.2 41.0 %copy-start.1 = (f32[64]{0:T(128)S(1)}, f32[64]{0:T(128)}, u32[]{:S(2)}) copy-start(f32[64]{0:T(128)} %get-tuple-element.7) | copy-start | bytes 772
  314.2 54.0 %copy-start.3 = (f32[64]{0:T(128)S(1)}, f32[64]{0:T(128)}, u32[]{:S(2)}) copy-start(f32[64]{0:T(128)} %copy-done.2) | copy-start | bytes 772
Sparse Core Ops, SparseCore 0:
  18.0 61.6 all-reduce.5
  89.8 43.0 all-reduce.7
  142.6 58.7 all-reduce.9
  257.3 43.4 all-reduce.11
  314.4 58.3 all-reduce.13
where the time goes:
time: 384 us; the launch traced here: 383 us
  waiting for transfers between devices  158 us (41%)
  blocking collectives  145 us (38%)
  matrix products  33.8 us (9%)
  other arithmetic  16.4 us (4%)
  local copies, waits for them, and re-layouts  15.9 us (4%)
  between operations  13.9 us (4%)
    psum x2, waiting for transfers between devices, per_device(): forward_image = lax.psum(forward_partial_value, 'col')  86.7 us
    psum x3, waiting for transfers between devices, backward(): return lax.psum(partial_value, 'row')  71 us
    psum x1, blocking collectives, per_device(): dir_norm = lax.psum(frame_product(direction, direction), ('row', 'col'))  40 us
    psum x1, blocking collectives, per_device(): norm_now = lax.psum(frame_product(residual, residual), ('row', 'col'))  39.8 us
    psum x1, blocking collectives, per_device(): norm_next = lax.psum(frame_product(residual, residual), ('row', 'col'))  39.7 us
    psum x2, blocking collectives, per_device(): image_norm = lax.psum(jnp.sum(forward_image * forward_image, axis=1), 'row')  25.8 us
    dot_general x3, matrix products, padded_apply(): jnp.einsum('fijr,ijmr->fjm', scaled, second_factor, preferred_element_typ...  19.5 us
    dot_general x2, matrix products, padded_apply(): jnp.einsum('fijr,ijsr->fis', scaled, second_factor, preferred_element_typ...  14.3 us
  transfers between devices with their start and end apart: 5, of which 5 were waited for; matrix products, arithmetic and copies ran while one was open for 0% of the time, Pallas kernels for 0%

commit v1 on v0

v1 whole, which is shorter than its diff:
```python
import functools

import jax
import jax.numpy as jnp
from jax import lax
from jax.experimental import pallas as pl
from jax.experimental.pallas import tpu as pltpu
from jax.sharding import PartitionSpec as P

GROUPS = 1

damping = 0.1
epsilon = 1e-06
MESH = pl.DeviceIdType.MESH
bf16 = jnp.bfloat16
f32 = jnp.float32


def lane_sums(value):
    total = value[:, 0:128]
    for start in range(128, value.shape[1], 128):
        total = total + value[:, start : start + 128]
    return total


def fold(value):
    return jnp.sum(value, axis=1, keepdims=True)


def kernel(sizes, u_hbm, v_hbm, scales, classes, slopes, x_ref, r_ref,
           u_vm, v_vm, wu, wv, hb, tb, pb, sib, hyp_s, hyp_r, full, own,
           sq, sq_r, hyq_s, hyq_r, csum, cs_s, cs_r, zb, zt, ch_s, ch_r, scal, own_scal,
           load_u, load_v, send_sem, recv_sem):
    R, C, G, TR, TC, T, K, F = sizes
    FG = F // G
    H = FG // 2
    phases = (R // 2).bit_length() - 1
    row = lax.axis_index("row")
    col = lax.axis_index("col")
    core = lax.rem(row, 2)
    chip = row // 2
    sibling = row + 1 - 2 * core

    def partner(bit):
        low = lax.rem(chip // (1 << bit), 2)
        return row + (1 - 2 * low) * (2 << bit)

    loads_u, loads_v = {}, {}
    for i in range(TR):
        for j in range(TC):
            loads_u[i, j] = pltpu.make_async_copy(
                u_hbm.at[i, j], u_vm.at[i, :, pl.ds(j * K, K)], load_u.at[i, j])
            loads_u[i, j].start()
    for j in range(TC):
        for i in range(TR):
            loads_v[i, j] = pltpu.make_async_copy(
                v_hbm.at[i, j], v_vm.at[j, :, pl.ds(i * K, K)], load_v.at[i, j])
            loads_v[i, j].start()

    barrier = pltpu.get_barrier_semaphore()
    pl.semaphore_signal(barrier, inc=1, device_id={"row": sibling}, device_id_type=MESH)
    for bit in range(phases):
        pl.semaphore_signal(barrier, inc=1, device_id={"row": partner(bit)}, device_id_type=MESH)

    @pl.when(col > 0)
    def _():
        pl.semaphore_signal(barrier, inc=1, device_id={"col": col - 1}, device_id_type=MESH)

    @pl.when(col < C - 1)
    def _():
        pl.semaphore_signal(barrier, inc=1, device_id={"col": col + 1}, device_id_type=MESH)

    lane = lax.broadcasted_iota(jnp.int32, (1, K), 1)
    least = ((lane >= K // 8).astype(jnp.int32) + (lane >= K // 4).astype(jnp.int32)
             + (lane >= K // 2).astype(jnp.int32))
    for i in range(TR):
        for j in range(TC):
            w = jnp.where(least <= classes[i, j], scales[i, j : j + 1, :], 0.0)
            wu[i : i + 1, j * K : (j + 1) * K] = w
            wv[j : j + 1, i * K : (i + 1) * K] = w

    @pl.when(col == 0)
    def _():
        for g in range(G):
            for a in range(2):
                ch_r[g, a, 0] = jnp.zeros_like(ch_r[g, a, 0])
                cs_r[g, a, 0] = jnp.zeros_like(cs_r[g, a, 0])

    @pl.when(col == C - 1)
    def _():
        for g in range(G):
            for a in range(2):
                ch_r[g, a, 1] = jnp.zeros_like(ch_r[g, a, 1])
                cs_r[g, a, 1] = jnp.zeros_like(cs_r[g, a, 1])

    count = [0]
    sent = []

    def ticket():
        count[0] += 1
        return count[0] - 1

    def remote(src, dst, number, device):
        return pltpu.make_async_remote_copy(
            src_ref=src, dst_ref=dst, send_sem=send_sem.at[number], recv_sem=recv_sem.at[number],
            device_id=device, device_id_type=MESH)

    mine = pl.ds(pl.multiple_of(core * H, H), H)
    theirs = pl.ds(pl.multiple_of((1 - core) * H, H), H)

    def push(src, dst, device):
        copy = remote(src, dst, ticket(), device)
        copy.start()
        sent.append((lambda: copy.wait_send(), None))
        return copy

    def chain(own_ref, s_ref, r_ref_, direction, number):
        up = (col > 0) if direction == 0 else (col < C - 1)
        down = (col < C - 1) if direction == 0 else (col > 0)
        to = lax.rem(col + 1, C) if direction == 0 else lax.rem(col + C - 1, C)

        def make():
            return remote(s_ref, r_ref_, number, {"col": to})

        @pl.when(up)
        def _():
            make().wait_recv()

        @pl.when(down)
        def _():
            s_ref[...] = (own_ref[...] + r_ref_[...].astype(f32)).astype(s_ref.dtype)
            make().start()

    def chain_all(own_ref, s_refs, r_refs, numbers, order):
        near = col < C // 2

        @pl.when(near)
        def _():
            chain(own_ref, s_refs[order], r_refs[order], order, numbers[order])

        @pl.when(jnp.logical_not(near))
        def _():
            chain(own_ref, s_refs[1 - order], r_refs[1 - order], 1 - order, numbers[1 - order])

    def note_chain(s_refs, r_refs, numbers):
        for d in range(2):
            def finish(d=d):
                remote(s_refs[d], r_refs[d], numbers[d], {"col": lax.rem(col + 1 + d * (C - 2), C)}).wait_send()
            sent.append((finish, (col < C - 1) if d == 0 else (col > 0)))

    first = [True] * (TR + TC)

    def h_stage(g, i, y):
        if first[i]:
            first[i] = False
            for j in range(TC):
                loads_u[i, j].wait()
        h = jnp.dot(y, u_vm[i], preferred_element_type=f32)
        h = (h * wu[i : i + 1, :]).astype(bf16)
        for j in range(TC):
            hb[g, j, :, i * K : (i + 1) * K] = h[:, j * K : (j + 1) * K]

    def t_stage(g, a, j):
        t = jnp.dot(full[g, a, :, j * T : (j + 1) * T], v_vm[j], preferred_element_type=f32)
        t = (t * wv[j : j + 1, :]).astype(bf16)
        for i in range(TR):
            tb[g, i, :, j * K : (j + 1) * K] = t[:, i * K : (i + 1) * K]

    def across(left, right):
        return lax.dot_general(left, right, (((1,), (1,)), ((), ())), preferred_element_type=f32)

    barrier_passed = [False]

    def process(g):
        frames = slice(g * FG, (g + 1) * FG)
        for i in range(TR):
            h_stage(g, i, slopes[frames, i * T : (i + 1) * T].astype(bf16))
        if not barrier_passed[0]:
            barrier_passed[0] = True
            pl.semaphore_wait(
                barrier, 1 + phases + (col > 0).astype(jnp.int32) + (col < C - 1).astype(jnp.int32))
        yield
        for a in range(3):
            yield from row_sum(g, a)
            if a < 2:
                yield from col_sum(g, a)

    def row_sum(g, a):
        copies = {}
        stages = phases + 3
        lags = [0, 2] + [2 + 3 * (n + 1) for n in range(phases)] + [4 + 3 * phases]

        def bit_of(j, n):
            return n if j % 2 == 0 else phases - 1 - n

        def cols(j):
            return pl.ds(j * T, T)

        def scalar_stage(k):
            q = a - 1
            if k == 0:
                copies["s", 0] = push(sq.at[g, q, theirs], sq_r.at[g, q], {"row": sibling})
            elif k <= phases + 1:
                copies["s", k - 1].wait_recv()
                if k == 1:
                    total = sq[g, q, mine] + sq_r[g, q]
                else:
                    total = hyq_s[g, q, k - 2] + hyq_r[g, q, k - 2]
                if k <= phases:
                    hyq_s[g, q, k - 1] = total
                    copies["s", k] = push(hyq_s.at[g, q, k - 1], hyq_r.at[g, q, k - 1], {"row": partner(k - 1)})
                else:
                    image_norm = fold(total)
                    now = scal[g, 0, mine] if a == 1 else scal[g, 1, mine]
                    now = now[:, 0:1]
                    if a == 1:
                        dir_norm = now
                    else:
                        rr0 = scal[g, 0, mine][:, 0:1]
                        beta = now / (rr0 + epsilon)
                        dir_norm = now + 2 * beta * scal[g, 2, mine][:, 0:1] + beta * beta * rr0
                        own_scal[g, 2] = jnp.broadcast_to(beta, (H, 128))
                    alpha = now / (image_norm + damping * dir_norm + epsilon)
                    own_scal[g, q] = jnp.broadcast_to(alpha, (H, 128))

        def finish(j, q):
            at = slice(j * T, (j + 1) * T)
            if a == 0:
                own[g, 0, :, at] = q
                full[g, 0, mine, at] = q.astype(bf16)
            elif a == 1:
                b = own[g, 0, :, at]
                res = b - own_scal[g, 0][:, 0:1] * (q + damping * b)
                own[g, 1, :, at] = res
                full[g, 1, mine, at] = res.astype(bf16)
            else:
                b = own[g, 0, :, at]
                res = own[g, 1, :, at]
                alpha0, alpha1, beta = (own_scal[g, n][:, 0:1] for n in range(3))
                direction = res + beta * b
                rows = pl.ds(pl.multiple_of(g * FG + core * H, H), H)
                x_ref[rows, at] = alpha0 * b + alpha1 * direction
                r_ref[rows, at] = res - alpha1 * (q + damping * direction)
                copies[j, "x"] = push(x_ref.at[rows, cols(j)], x_ref.at[rows, cols(j)], {"row": sibling})
                copies[j, "r"] = push(r_ref.at[rows, cols(j)], r_ref.at[rows, cols(j)], {"row": sibling})
                return
            copies[j, "g"] = push(full.at[g, a, mine, cols(j)], full.at[g, a, mine, cols(j)], {"row": sibling})

        def stage(j, k):
            at = slice(j * T, (j + 1) * T)
            if k == 0:
                if first[TR + j]:
                    first[TR + j] = False
                    for i in range(TR):
                        loads_v[i, j].wait()
                pb[g, a, :, at] = across(hb[g, j], v_vm[j])
                copies[j, 0] = push(pb.at[g, a, theirs, cols(j)], sib.at[g, a, :, cols(j)], {"row": sibling})
            elif k <= phases + 1:
                copies[j, k - 1].wait_recv()
                if k == 1:
                    total = pb[g, a, mine, at] + sib[g, a, :, at]
                else:
                    total = hyp_s[g, a, k - 2, :, at].astype(f32) + hyp_r[g, a, k - 2, :, at].astype(f32)
                if k <= phases:
                    hyp_s[g, a, k - 1, :, at] = total.astype(bf16)
                    copies[j, k] = push(hyp_s.at[g, a, k - 1, :, cols(j)], hyp_r.at[g, a, k - 1, :, cols(j)],
                                        {"row": partner(bit_of(j, k - 1))})
                else:
                    finish(j, total)
            elif a == 2:
                copies[j, "x"].wait_recv()
                copies[j, "r"].wait_recv()
            else:
                copies[j, "g"].wait_recv()
                t_stage(g, a, j)
                now = full[g, a, :, at].astype(f32)
                terms = [lane_sums(now * now)]
                if a == 1:
                    terms.append(lane_sums(now * full[g, 0, :, at].astype(f32)))
                for n, term in enumerate(terms):
                    csum[g, a, n] = term if j == 0 else csum[g, a, n] + term

        for slot in range(TC + lags[-1]):
            for k in range(stages - 1, 0, -1):
                if a > 0 and slot == lags[k] and k <= phases + 1:
                    scalar_stage(k)
                if 0 <= slot - lags[k] < TC:
                    stage(slot - lags[k], k)
            if a > 0 and slot == 0:
                scalar_stage(0)
            if slot < TC:
                stage(slot, 0)
            yield

    def col_sum(g, a):
        numbers = [(ticket(), ticket()) for _ in range(TR + 1)]
        n_sums = 1 + a
        part = pl.ds(0, n_sums)

        def refs(i):
            if i < 0:
                return (csum.at[g, a, part], [cs_s.at[g, a, d, part] for d in range(2)],
                        [cs_r.at[g, a, d, part] for d in range(2)])
            at = pl.ds(i * T, T)
            return (zb.at[g, a, :, at], [ch_s.at[g, a, d, :, at] for d in range(2)],
                    [ch_r.at[g, a, d, :, at] for d in range(2)])

        edge = jnp.logical_or(col == 0, col == C - 1)

        def stage(i, k):
            own_ref, s_refs, r_refs = refs(i)
            if k == 0:
                if i >= 0:
                    zb[g, a, :, i * T : (i + 1) * T] = across(tb[g, i], u_vm[i])
                note_chain(s_refs, r_refs, numbers[i])

                @pl.when(edge)
                def _():
                    chain_all(own_ref, s_refs, r_refs, numbers[i], 0)
            elif k == 1:
                @pl.when(jnp.logical_not(edge))
                def _():
                    chain_all(own_ref, s_refs, r_refs, numbers[i], 0)
            elif k == 2:
                chain_all(own_ref, s_refs, r_refs, numbers[i], 1)
            elif i < 0:
                for n in range(n_sums):
                    total = csum[g, a, n] + cs_r[g, a, 0, n] + cs_r[g, a, 1, n]
                    scal[g, a + n] = jnp.broadcast_to(fold(total), (FG, 128))
            else:
                at = slice(i * T, (i + 1) * T)
                z = zb[g, a, :, at] + ch_r[g, a, 0, :, at].astype(f32) + ch_r[g, a, 1, :, at].astype(f32)
                if a == 0:
                    zt[g, :, at] = z
                else:
                    beta = scal[g, 1][:, 0:1] / (scal[g, 0][:, 0:1] + epsilon)
                    z = z + beta * zt[g, :, at]
                term = lane_sums(z * z)
                sq[g, a] = term if i == 0 else sq[g, a] + term
                h_stage(g, i, z.astype(bf16))

        lags = [0, 1, 2, 3]
        for slot in range(TR + lags[-1] + 1):
            for k in range(3, -1, -1):
                if slot == max(lags[k], 0):
                    stage(-1, k)
                if 0 <= slot - lags[k] < TR:
                    stage(slot - lags[k], k)
            yield

    running = [process(g) for g in range(G)]
    ahead = 20
    for _ in range(ahead if G > 1 else 0):
        next(running[0])
    while running:
        for one in list(running):
            try:
                next(one)
            except StopIteration:
                running.remove(one)

    for finish, condition in sent:
        if condition is None:
            finish()
        else:
            pl.when(condition)(finish)


def per_device(u_factors, v_factors, tile_scales, rank_class, slopes):
    R, C, G = lax.axis_size("row"), lax.axis_size("col"), GROUPS
    TR, TC, T, K = u_factors.shape
    F = slopes.shape[0]
    FG, H = F // G, F // G // 2
    NM, NS = TC * T, TR * T
    phases = (R // 2).bit_length() - 1
    copies = G * (3 * (TC * (2 + phases)) + TC + 2 * (1 + phases) + 2 * 2 * (TR + 1))
    vm = pltpu.VMEM
    scratch = [
        vm((TR, T, TC * K), bf16), vm((TC, T, TR * K), bf16),
        vm((TR, TC * K), f32), vm((TC, TR * K), f32),
        vm((G, TC, FG, TR * K), bf16), vm((G, TR, FG, TC * K), bf16),
        vm((G, 3, FG, NM), f32), vm((G, 3, H, NM), f32),
        vm((G, 3, phases, H, NM), bf16), vm((G, 3, phases, H, NM), bf16),
        vm((G, 2, FG, NM), bf16), vm((G, 2, H, NM), f32),
        vm((G, 2, FG, 128), f32), vm((G, 2, H, 128), f32),
        vm((G, 2, phases, H, 128), f32), vm((G, 2, phases, H, 128), f32),
        vm((G, 2, 2, FG, 128), f32), vm((G, 2, 2, 2, FG, 128), f32), vm((G, 2, 2, 2, FG, 128), f32),
        vm((G, 2, FG, NS), f32), vm((G, FG, NS), f32),
        vm((G, 2, 2, FG, NS), bf16), vm((G, 2, 2, FG, NS), bf16),
        vm((G, 3, FG, 128), f32), vm((G, 3, H, 128), f32),
        pltpu.SemaphoreType.DMA((TR, TC)), pltpu.SemaphoreType.DMA((TR, TC)),
        pltpu.SemaphoreType.DMA((copies,)), pltpu.SemaphoreType.DMA((copies,)),
    ]
    out = jax.ShapeDtypeStruct((F, NM), f32)
    return pl.pallas_call(
        functools.partial(kernel, (R, C, G, TR, TC, T, K, F)),
        out_shape=(out, out),
        in_specs=[
            pl.BlockSpec(memory_space=pl.ANY), pl.BlockSpec(memory_space=pl.ANY),
            pl.BlockSpec(memory_space=pltpu.VMEM), pl.BlockSpec(memory_space=pltpu.SMEM),
            pl.BlockSpec(memory_space=pltpu.VMEM),
        ],
        out_specs=[pl.BlockSpec(memory_space=pltpu.VMEM)] * 2,
        scratch_shapes=scratch,
        compiler_params=pltpu.CompilerParams(
            collective_id=0, has_side_effects=True, vmem_limit_bytes=56 * 2**20),
    )(u_factors, v_factors, tile_scales, rank_class, slopes)


def solution(mesh):
    return jax.shard_map(
        per_device,
        mesh=mesh,
        in_specs=(
            P("row", "col", None, None),
            P("row", "col", None, None),
            P("row", "col", None),
            P("row", "col"),
            P(None, "row"),
        ),
        out_specs=(P(None, "col"), P(None, "col")),
        check_vma=False,
    )
```

time: 384 us -> 125 us (0.33)
  waiting for transfers between devices: 158 us -> 0 us
  blocking collectives: 145 us -> 0 us
  Pallas kernels: 0 us -> 120 us
  matrix products: 33.8 us -> 0 us
  other arithmetic: 16.4 us -> 0 us
  between operations: 13.9 us -> 0.65 us
  local copies, waits for them, and re-layouts: 15.9 us -> 3.93 us
    psum x5 -> x0, waiting for transfers between devices: 158 us -> none  [the longest x2 86.7 us: per_device(): forward_image = lax.psum(forward_partial_value, 'col')]
    psum x5 -> x0, blocking collectives: 145 us -> none  [the longest x1 40 us: per_device(): dir_norm = lax.psum(frame_product(direction, direction), ('row', 'col'))]
    pallas_call x0 -> x1, Pallas kernels: none -> 120 us  [per_device(): pl.pallas_call(functools.partial(kernel, (R, C, G, TR, TC, T, K, F)), out...]
    dot_general x5 -> x0, matrix products: 33.8 us -> none  [the longest x3 19.5 us: padded_apply(): jnp.einsum('fijr,ijmr->fjm', scaled, second_factor, preferred_element_typ...]
    reshape x10 -> x0, local copies, waits for them, and re-layouts: 14.6 us -> none  [the longest x3 5.37 us: padded_apply(): return result.reshape(frames, cols_here * tile_size)]
    convert_element_type x4 -> x0, other arithmetic: 6.41 us -> none  [the longest x2 3.16 us: per_device(): narrowed = direction.astype(jnp.bfloat16)]
    sub x2 -> x0, other arithmetic: 5.68 us -> none  [per_device(): residual = residual - step_size[:, None] * operator_image]
  transfers between devices with their start and end apart: 5 -> 0, of which waited for: 5 -> 0; matrix products, arithmetic and copies ran while one was open for 0% -> 0% of each run, Pallas kernels for 0% -> 0%
where the time goes in v1:
time: 125 us
  Pallas kernels  120 us (96%)
  local copies, waits for them, and re-layouts  3.93 us (3%)
    pallas_call x1, Pallas kernels, per_device(): pl.pallas_call(functools.partial(kernel, (R, C, G, TR, TC, T, K, F)), out...  120 us
    unnamed x4, local copies, waits for them, and re-layouts  3.93 us

profile of v1, /device:TPU:0, one launch (start us, length us, event | category | flops | bytes accessed | tf_op | source)
XLA Modules:
  0.0 125.0 jit_solution(17677520224196077753)
XLA Ops:
  0.6 120.4 %shard_map.68 = (f32[64,6144]{1,0:T(8,128)}, f32[64,6144]{1,0:T(8,128)}) custom-call(bf16[3,6,1024,128]{3,2,1,0:T(8,128)(2,1)} %u_hbm.1, bf16[3,6,1024,128]{3,2,1,0:T(8,128)(2,1)} %v_hbm.1, f32[3,6,128]{2,1,0:T(8,128)} %scales.1, s32[3,6]{1,0:T(4,128)} %classes.1, f32[64,3072]{1,0:T(8,128)} %slopes.1), custom_call_target="tpu_custom_call" | custom-call | tf_op jit(solution)/shard_map/pallas_call | solution.py:395
  121.0 0.0 copy-start
  121.1 2.8 %copy.9 = f32[64,6144]{1,0:T(8,128)} copy(f32[64,6144]{1,0:T(8,128)} %get-tuple-element.4) | data formatting | bytes 3145728
  123.8 0.0 copy-done
  123.8 1.1 copy.10
Async XLA Ops:
  121.0 2.8 %copy-start = (f32[64,6144]{1,0:T(8,128)S(1)}, f32[64,6144]{1,0:T(8,128)}, u32[]{:S(2)}) copy-start(f32[64,6144]{1,0:T(8,128)} %get-tuple-element.5) | copy-start | bytes 4718596
